TPU v7x, 768 devices: a whole 4x8x12 slice. The times are simulated.
768 devices in a mesh: space: 12 (over z), help: 32 (over x, y), chan: 2 (over core).
Axes of the slice: x: 4, y: 8, z: 12, core: 2. Of those that a mesh axis runs over, the one named last changes fastest.
Arguments:
- node_feats: bfloat16 [12288, 49, 128], P(('space', 'help'), None, 'chan'), may hold values from -6 to 6
- source_index: int32 [1536, 128], P(('space', 'help')), may hold values from 0 to 287
- target_index: int32 [1536, 128], P(('space', 'help')), may hold values from 0 to 31
- edge_angle: float32 [1536, 128], P(('space', 'help')), may hold values from -3.140625 to 3.140625
- edge_envelope: float32 [1536, 128], P(('space', 'help')), may hold values from 0.1 to 1
- live_blocks: int32 [384], P(('space', 'help')), may hold values from 0 to 4, as said below
- w_zero: bfloat16 [7, 128, 896], replicated, may hold values from -0.1875 to 0.1875
- w_one: bfloat16 [2, 6, 128, 768], replicated, may hold values from -0.15625 to 0.15625
- w_two: bfloat16 [2, 5, 128, 640], replicated, may hold values from -0.15625 to 0.15625
Outputs:
- messages: bfloat16 [12288, 29, 128], P(('space', 'help'), None, 'chan')
Inputs may be any that keep to these rules, and one draw needn't show every extreme that they name: A domain's live edge blocks are the first live_blocks of its 4 slots; edges in the other slots contribute nothing; some domain has all 4 live. `source_index`: index // 32 = 3 (ds + 1) + (dh + 1) names the domain at offset ds along space and dh along help, index % 32 an atom of it.
All inputs are finite; a program needn't handle non-finite values.
Results may differ from a plain program's by a relative error of at most 0.0065.
Values may be sent and summed in bfloat16 or wider, within the bound.
A program may use at most 64 MiB of HBM per device.

v0:
```python
import jax
import jax.numpy as jnp
import numpy as np
from jax import lax
from jax.sharding import PartitionSpec as P

LMAX = 6


def with_halo(cells, sides, width):
    for axis, dim in sides:
        count = lax.axis_size(axis)
        ends = count - 1
        head = lax.slice_in_dim(cells, 0, width, axis=dim)
        tail = lax.slice_in_dim(cells, cells.shape[dim] - width, cells.shape[dim], axis=dim)
        cells = jnp.concatenate(
            [
                lax.ppermute(tail, axis, [(i, (i + 1) % count) for i in range(ends)]),
                cells,
                lax.ppermute(head, axis, [((i + 1) % count, i) for i in range(ends)]),
            ],
            axis=dim,
        )
    return cells


def coefficient_order(top_degree):
    order_list = [degree * degree + degree for degree in range(top_degree + 1)]
    for order_m in (1, 2):
        order_list += [
            degree * degree + degree + order_m for degree in range(order_m, top_degree + 1)
        ]
        order_list += [
            degree * degree + degree - order_m for degree in range(order_m, top_degree + 1)
        ]
    return np.array(order_list, dtype=np.int32)


def turn_edges(features, edge_turn, direction, top_degree):
    count_zero, count_one, count_two = (top_degree + 1, top_degree, top_degree - 1)
    cos_one = jnp.cos(edge_turn)[:, None, None]
    sin_one = direction * jnp.sin(edge_turn)[:, None, None]
    cos_two = jnp.cos(2.0 * edge_turn)[:, None, None]
    sin_two = direction * jnp.sin(2.0 * edge_turn)[:, None, None]
    base_two = count_zero + 2 * count_one
    order_zero = features[:, :count_zero]
    plus_one = features[:, count_zero : count_zero + count_one]
    minus_one = features[:, count_zero + count_one : base_two]
    plus_two = features[:, base_two : base_two + count_two]
    minus_two = features[:, base_two + count_two :]
    return jnp.concatenate(
        [
            order_zero,
            cos_one * plus_one + sin_one * minus_one,
            cos_one * minus_one - sin_one * plus_one,
            cos_two * plus_two + sin_two * minus_two,
            cos_two * minus_two - sin_two * plus_two,
        ],
        axis=1,
    )


def mix_orders(rotated, weight_set, top_degree):
    count_zero, count_one, count_two = (top_degree + 1, top_degree, top_degree - 1)
    edge_count = rotated.shape[0]
    in_width = rotated.shape[2]
    zero_weight, one_real, one_imag, two_real, two_imag = weight_set
    out_width = zero_weight.shape[1] // count_zero

    def flatten(lower, upper):
        return rotated[:, lower:upper].reshape(edge_count, (upper - lower) * in_width)

    def product(left, right):
        return jnp.dot(left, right, preferred_element_type=jnp.float32)

    base_two = count_zero + 2 * count_one
    plus_one = flatten(count_zero, count_zero + count_one)
    minus_one = flatten(count_zero + count_one, base_two)
    plus_two = flatten(base_two, base_two + count_two)
    minus_two = flatten(base_two + count_two, base_two + 2 * count_two)
    pieces = [
        (product(flatten(0, count_zero), zero_weight), count_zero),
        (product(plus_one, one_real) - product(minus_one, one_imag), count_one),
        (product(plus_one, one_imag) + product(minus_one, one_real), count_one),
        (product(plus_two, two_real) - product(minus_two, two_imag), count_two),
        (product(plus_two, two_imag) + product(minus_two, two_real), count_two),
    ]
    return jnp.concatenate(
        [piece.reshape(edge_count, rows, out_width) for piece, rows in pieces], axis=1
    )


def input_rows(weight, chan_start, half_width):
    degrees, full_width = (weight.shape[0], weight.shape[1])
    picked = lax.dynamic_slice_in_dim(weight, chan_start, half_width, 1)
    return picked.reshape(degrees * half_width, degrees * full_width)


def shards(
    node_feats,
    source_index,
    target_index,
    edge_angle,
    edge_envelope,
    live_blocks,
    w_zero,
    w_one,
    w_two,
):
    order_list = coefficient_order(LMAX)
    own_feats = node_feats[:, order_list, :]
    half_width = own_feats.shape[2]
    atom_count = own_feats.shape[0]
    trunc_count = own_feats.shape[1]
    chan_start = lax.axis_index("chan") * half_width
    raw_weights = (w_zero, w_one[0], w_one[1], w_two[0], w_two[1])
    weight_set = tuple((input_rows(weight, chan_start, half_width) for weight in raw_weights))
    in_width = own_feats.shape[2]
    out_width = weight_set[0].shape[1] // (LMAX + 1)
    nearby = with_halo(own_feats[None, None], (("space", 0), ("help", 1)), 1)
    nearby = nearby.reshape(9 * atom_count, trunc_count, in_width)
    atom_ids = jnp.arange(atom_count, dtype=jnp.int32)

    def block_term(rotated, envelope, targets):
        mixed = mix_orders(rotated, weight_set, LMAX)
        message = mixed * envelope[:, None, None]
        flat_msg = message.reshape(message.shape[0], trunc_count * out_width)
        upper_part = lax.optimization_barrier(flat_msg.astype(jnp.bfloat16))
        lower_part = (flat_msg - upper_part.astype(jnp.float32)).astype(jnp.bfloat16)
        onehot = (targets[None, :] == atom_ids[:, None]).astype(jnp.bfloat16)
        summed = jnp.dot(onehot, upper_part, preferred_element_type=jnp.float32) + jnp.dot(
            onehot, lower_part, preferred_element_type=jnp.float32
        )
        return summed.reshape(atom_count, trunc_count, out_width)

    def rotate_block(block_id):
        picked = jnp.take(nearby, source_index[block_id], axis=0)
        return turn_edges(picked.astype(jnp.float32), edge_angle[block_id], 1.0, LMAX).astype(
            jnp.bfloat16
        )

    def own_step(block_id, running):
        return running + block_term(
            rotate_block(block_id), edge_envelope[block_id], target_index[block_id]
        )

    empty = jnp.zeros((atom_count, trunc_count, out_width), jnp.float32)
    live_count = live_blocks[0]
    running = lax.fori_loop(0, live_count, own_step, empty)
    result = lax.psum_scatter(running, "chan", scatter_dimension=2, tiled=True)
    return result.astype(jnp.bfloat16)


def solution(mesh):
    in_specs = (
        P(("space", "help"), None, "chan"),
        P(("space", "help"), None),
        P(("space", "help"), None),
        P(("space", "help"), None),
        P(("space", "help"), None),
        P(("space", "help")),
        P(),
        P(),
        P(),
    )
    out_specs = P(("space", "help"), None, "chan")
    return jax.shard_map(shards, mesh=mesh, in_specs=in_specs, out_specs=out_specs, check_vma=False)
```

profile of v0, /device:TPU:1, one launch (start us, length us, event | category | flops | bytes accessed | tf_op | source)
XLA Modules:
  0.0 196.0 jit_solution(16276051665939312620)
XLA Ops:
  6.5 0.0 copy-start
  6.5 0.8 pad_clamp_fusion.1
  7.3 1.6 gather_fusion.1
  8.9 0.0 copy-start.14
  8.9 1.4 collective-permute-start.1
  10.4 6.2 %collective-permute-start = (bf16[1,1,32,29,64]{4,2,3,1,0:T(8,128)(2,1)S(1)}, bf16[1,1,32,29,64]{4,2,3,1,0:T(8,128)(2,1)}, u32[]{:S(2)}, u32[]{:S(2)}) collective-permute-start(bf16[1,1,32,29,64]{4,2,3,1,0:T(8,128)(2,1)S(1)} %bitcast.173), channel_id=1, source_target_pairs={{0,64},{64,128},{128,192},{192,256},{256,320},{320,384},{384,448},... | collective-permute-start | bytes 356360 | tf_op jit(solution)/shard_map/ppermute | solution.py:18
  16.5 2.8 %fusion.12 = (bf16[1,6,128,768]{3,2,1,0:T(8,128)(2,1)S(1)}, bf16[1,6,128,768]{3,2,1,0:T(8,128)(2,1)}) fusion(bf16[2,6,128,768]{3,2,1,0:T(8,128)(2,1)} %param.20), kind=kLoop, calls=%fused_computation.51 | loop fusion | bytes 4718592 | tf_op jit(solution)/shard_map/slice | solution.py:116
  19.4 0.0 copy-done.14
  19.4 1.3 fusion.13
  20.7 0.0 collective-permute-done.1
  20.7 0.0 collective-permute-done
  20.7 1.2 pad_maximum_fusion.1
  22.0 1.4 collective-permute-start.3
  23.4 4.0 %collective-permute-start.2 = (bf16[3,1,32,29,64]{4,2,3,1,0:T(8,128)(2,1)S(1)}, bf16[3,1,32,29,64]{4,2,3,1,0:T(8,128)(2,1)S(1)}, u32[]{:S(2)}, u32[]{:S(2)}) collective-permute-start(bf16[3,1,32,29,64]{4,2,3,1,0:T(8,128)(2,1)S(1)} %pad_maximum_fusion.1), channel_id=1, source_target_pairs={{0,2},{2,4},{4,6},{6,8},{8,10},{10,12},{12,14},{14,16},{16,18},{18... | collective-permute-start | bytes 1069064 | tf_op jit(solution)/shard_map/ppermute | solution.py:18
  27.5 1.0 constant_dynamic-slice_fusion.8
  28.5 0.0 copy-done.12
  28.5 1.0 constant_dynamic-slice_fusion.4
  29.5 0.0 copy-done.9
  29.5 0.9 constant_dynamic-slice_fusion.6
  30.4 3.7 %collective-permute-done.3 = bf16[3,1,32,29,64]{4,2,3,1,0:T(8,128)(2,1)S(1)} collective-permute-done((bf16[3,1,32,29,64]{4,2,3,1,0:T(8,128)(2,1)S(1)}, bf16[3,1,32,29,64]{4,2,3,1,0:T(8,128)(2,1)S(1)}, u32[]{:S(2)}, u32[]{:S(2)}) %collective-permute-start.3) | collective-permute-done | bytes 356384 | tf_op jit(solution)/shard_map/ppermute | solution.py:20
  34.1 1.5 collective-permute-done.2
  35.6 1.6 pad_maximum_fusion
  37.1 0.0 copy-start.17
  37.2 2.4 %copy.57 = bf16[3,3,32,29,64]{4,3,2,1,0:T(8,128)(2,1)} copy(bf16[3,3,32,29,64]{4,2,3,1,0:T(8,128)(2,1)S(1)} %pad_maximum_fusion) | data formatting | bytes 2138112 | tf_op jit(solution)/shard_map/concatenate | solution.py:16
  39.5 0.9 broadcast_in_dim.24
  40.4 0.7 while.11
  41.1 3.8 %copy.59 = f32[32,29,128]{0,1,2:T(8,128)} copy(f32[32,29,128]{2,1,0:T(8,128)} %get-tuple-element.78) | data formatting | bytes 950272
  44.9 3.0 %reshape.158 = f32[128,928]{1,0:T(8,128)} reshape(f32[128,29,32]{2,1,0:T(8,128)} %bitcast.170) | data formatting | bytes 950272
  47.9 0.0 reduce-scatter.4.cloned.1.call-update
  47.9 138.6 %reduce-scatter.4.cloned.1.call-done = f32[64,928]{1,0:T(8,128)} async-done(((f32[128,928]{1,0:T(8,128)}), f32[64,928]{1,0:T(8,128)}) %reduce-scatter.4.cloned.1.call-update) | async-done | bytes 237584
  186.5 1.4 reshape.159
  187.9 1.2 copy.60
  (15 shorter events, 0.0 us)
Async XLA Ops:
  6.5 20.9 %copy-start = (bf16[7,128,896]{2,1,0:T(8,128)(2,1)S(1)}, bf16[7,128,896]{2,1,0:T(8,128)(2,1)}, u32[]{:S(2)}) copy-start(bf16[7,128,896]{2,1,0:T(8,128)(2,1)} %param.19) | copy-start | bytes 4816900
  6.5 180.0 %reduce-scatter.4.cloned.1.call-start = ((), (), s32[]{:S(2)}) async-start(), calls=%async_computation.1 | async-start | bytes 786432
  8.9 11.8 %copy-start.10 = (bf16[29,32,64]{2,1,0:T(8,128)(2,1)}, bf16[29,32,64]{2,1,0:T(8,128)(2,1)S(1)}, u32[]{:S(2)}) copy-start(bf16[29,32,64]{2,1,0:T(8,128)(2,1)S(1)} %gather_fusion.1) | copy-start | bytes 356356
  8.9 10.4 %copy-start.14 = (bf16[2,5,128,640]{3,2,1,0:T(8,128)(2,1)S(1)}, bf16[2,5,128,640]{3,2,1,0:T(8,128)(2,1)}, u32[]{:S(2)}) copy-start(bf16[2,5,128,640]{3,2,1,0:T(8,128)(2,1)} %param.21) | copy-start | bytes 4915204
  8.9 11.8 %collective-permute-start.1 = (bf16[1,1,32,29,64]{4,2,3,1,0:T(8,128)(2,1)S(1)}, bf16[1,1,32,29,64]{4,2,3,1,0:T(8,128)(2,1)S(1)}, u32[]{:S(2)}, u32[]{:S(2)}) collective-permute-start(bf16[1,1,32,29,64]{4,2,3,1,0:T(8,128)(2,1)S(1)} %bitcast.172), channel_id=1, source_target_pairs={{64,0},{128,64},{192,128},{256,192},{320,256},{384,320},{448,384},... | collective-permute-start | bytes 356360 | tf_op jit(solution)/shard_map/ppermute | solution.py:20
  10.4 10.4 %collective-permute-start = (bf16[1,1,32,29,64]{4,2,3,1,0:T(8,128)(2,1)S(1)}, bf16[1,1,32,29,64]{4,2,3,1,0:T(8,128)(2,1)}, u32[]{:S(2)}, u32[]{:S(2)}) collective-permute-start(bf16[1,1,32,29,64]{4,2,3,1,0:T(8,128)(2,1)S(1)} %bitcast.173), channel_id=1, source_target_pairs={{0,64},{64,128},{128,192},{192,256},{256,320},{320,384},{384,448},... | collective-permute-start | bytes 356360 | tf_op jit(solution)/shard_map/ppermute | solution.py:18
  20.7 7.8 %copy-start.12 = (bf16[1,5,128,640]{3,2,1,0:T(8,128)(2,1)S(1)}, bf16[1,5,128,640]{3,2,1,0:T(8,128)(2,1)}, u32[]{:S(2)}) copy-start(bf16[1,5,128,640]{3,2,1,0:T(8,128)(2,1)} %get-tuple-element.147) | copy-start | bytes 2457604
  20.7 7.8 %copy-start.13 = (bf16[1,5,128,640]{3,2,1,0:T(8,128)(2,1)S(1)}, bf16[1,5,128,640]{3,2,1,0:T(8,128)(2,1)}, u32[]{:S(2)}) copy-start(bf16[1,5,128,640]{3,2,1,0:T(8,128)(2,1)} %get-tuple-element.148) | copy-start | bytes 2457604
  20.7 8.7 %copy-start.15 = (bf16[1,1,32,29,64]{4,2,3,1,0:T(8,128)(2,1)}, bf16[1,1,32,29,64]{4,2,3,1,0:T(8,128)(2,1)S(1)}, u32[]{:S(2)}) copy-start(bf16[1,1,32,29,64]{4,2,3,1,0:T(8,128)(2,1)S(1)} %collective-permute-done.1) | copy-start | bytes 356356
  22.0 7.5 %copy-start.9 = (bf16[1,6,128,768]{3,2,1,0:T(8,128)(2,1)S(1)}, bf16[1,6,128,768]{3,2,1,0:T(8,128)(2,1)}, u32[]{:S(2)}) copy-start(bf16[1,6,128,768]{3,2,1,0:T(8,128)(2,1)} %get-tuple-element.146) | copy-start | bytes 3538948
  22.0 12.1 %collective-permute-start.3 = (bf16[3,1,32,29,64]{4,2,3,1,0:T(8,128)(2,1)S(1)}, bf16[3,1,32,29,64]{4,2,3,1,0:T(8,128)(2,1)S(1)}, u32[]{:S(2)}, u32[]{:S(2)}) collective-permute-start(bf16[3,1,32,29,64]{4,2,3,1,0:T(8,128)(2,1)S(1)} %pad_maximum_fusion.1), channel_id=1, source_target_pairs={{2,0},{4,2},{6,4},{8,6},{10,8},{12,10},{14,12},{16,14},{18,16},{20... | collective-permute-start | bytes 1069064 | tf_op jit(solution)/shard_map/ppermute | solution.py:20
  23.4 12.1 %collective-permute-start.2 = (bf16[3,1,32,29,64]{4,2,3,1,0:T(8,128)(2,1)S(1)}, bf16[3,1,32,29,64]{4,2,3,1,0:T(8,128)(2,1)S(1)}, u32[]{:S(2)}, u32[]{:S(2)}) collective-permute-start(bf16[3,1,32,29,64]{4,2,3,1,0:T(8,128)(2,1)S(1)} %pad_maximum_fusion.1), channel_id=1, source_target_pairs={{0,2},{2,4},{4,6},{6,8},{8,10},{10,12},{12,14},{14,16},{16,18},{18... | collective-permute-start | bytes 1069064 | tf_op jit(solution)/shard_map/ppermute | solution.py:18
  28.5 7.1 %copy-start.11 = (bf16[29,32,64]{2,1,0:T(8,128)(2,1)S(1)}, bf16[29,32,64]{2,1,0:T(8,128)(2,1)}, u32[]{:S(2)}) copy-start(bf16[29,32,64]{2,1,0:T(8,128)(2,1)} %copy-done.10) | copy-start | bytes 356356
  29.5 6.1 %copy-start.16 = (bf16[1,1,32,29,64]{4,2,3,1,0:T(8,128)(2,1)S(1)}, bf16[1,1,32,29,64]{4,2,3,1,0:T(8,128)(2,1)}, u32[]{:S(2)}) copy-start(bf16[1,1,32,29,64]{4,2,3,1,0:T(8,128)(2,1)} %copy-done.15) | copy-start | bytes 356356
  37.1 3.3 %copy-start.17 = (s32[4,128]{1,0:T(4,128)S(1)}, s32[4,128]{1,0:T(4,128)}, u32[]{:S(2)}) copy-start(s32[4,128]{1,0:T(4,128)} %param.14) | copy-start | bytes 6148
Sparse Core Ops, SparseCore 0:
  48.1 138.3 reduce-scatter.3
where the time goes:
time: 198 us; the launch traced here: 196 us
  waiting for transfers between devices  144 us (73%)
  local copies, waits for them, and re-layouts  21.4 us (11%)
  between operations  13.5 us (7%)
  starting transfers between devices  13.1 us (7%)
  other arithmetic  3.6 us (2%)
    unnamed x2, waiting for transfers between devices  139 us
    ppermute x2, starting transfers between devices, with_halo(): lax.ppermute(tail, axis, [(i, (i + 1) % count) for i in range(ends)])  10.2 us
    unnamed x24, local copies, waits for them, and re-layouts  9.52 us
    slice x2, local copies, waits for them, and re-layouts, shards(): raw_weights = (w_zero, w_one[0], w_one[1], w_two[0], w_two[1])  4.17 us
  transfers between devices with their start and end apart: 5, of which 3 were waited for; matrix products, arithmetic and copies ran while one was open for 4% of the time, Pallas kernels for 0%

commit v1 on v0

v1 whole, which is shorter than its diff:
```python
import functools

import jax
import jax.numpy as jnp
from jax import lax
from jax.experimental import pallas as pl
from jax.experimental.pallas import tpu as pltpu
from jax.sharding import PartitionSpec as P

MESH = pl.DeviceIdType.MESH
F32, BF16 = jnp.float32, jnp.bfloat16
ATOMS = 32
HALF = 64
ROW = 3 * ATOMS

PLUS_ONE = [l * l + l + 1 for l in range(1, 7)]
MINUS_ONE = [l * l + l - 1 for l in range(1, 7)]
PLUS_TWO = [l * l + l + 2 for l in range(2, 7)]
MINUS_TWO = [l * l + l - 2 for l in range(2, 7)]
ZERO = [l * l + l for l in range(7)]
PACK = (
    PLUS_ONE + MINUS_ONE,
    PLUS_TWO[:4] + MINUS_TWO[:4] + [PLUS_TWO[4], MINUS_TWO[4]],
    ZERO + ZERO[-1:],
)
WIDTH = tuple(HALF * len(order) for order in PACK)
SUMS = ((2 * ATOMS, 768), (2 * ATOMS, 640), (ATOMS, 896))
OUT_AT = ((7, 12), (19, 10), (0, 7))


def dot(a, b):
    return jnp.dot(a, b, preferred_element_type=F32)


def kernel(
    n_space, n_help,
    x_hbm, src_hbm, tgt_hbm, ang_hbm, env_hbm, live_hbm, w0_hbm, w1_hbm, w2_hbm,
    out_ref,
    src_ref, tgt_ref, ang_ref, env_ref, live_ref, xv, rx_one, rx_two, rx_zero, edges, edges_in,
    tx_one, tx_two, tx_zero, in_one, in_two, in_zero,
    wv_one, wv_two, wv_zero, give,
    in_sem, w_sem, halo_send, halo_recv, edge_send, edge_recv,
    sum_send, sum_recv, out_send, out_recv,
):
    s, h, c = lax.axis_index("space"), lax.axis_index("help"), lax.axis_index("chan")
    has_help = (h > 0, h < n_help - 1)
    has_space = (s > 0, s < n_space - 1)
    rx = (rx_one, rx_two, rx_zero)
    tx = (tx_one, tx_two, tx_zero)
    sums_in = (in_one, in_two, in_zero)
    partner = (s, h, 1 - c)

    barrier = pltpu.get_barrier_semaphore()

    def greet(device):
        pl.semaphore_signal(barrier, inc=1, device_id=device, device_id_type=MESH)

    greet(partner)
    for side in range(2):
        step = 2 * side - 1

        @pl.when(has_help[side])
        def _():
            greet((s, h + step, 0))
            greet((s, h + step, 1))

        @pl.when(has_space[side])
        def _():
            greet((s + step, h, c))

    loads = [
        pltpu.make_async_copy(source, held, in_sem.at[at])
        for at, (source, held) in enumerate((
            (x_hbm, xv), (src_hbm, src_ref), (tgt_hbm, tgt_ref), (ang_hbm, ang_ref),
            (env_hbm, env_ref), (live_hbm, live_ref),
        ))
    ]
    for load in loads:
        load.start()

    def weight_copies(role):
        if role == 0:
            return [
                pltpu.make_async_copy(
                    w1_hbm.at[part, :, pl.ds(half * HALF, HALF)], wv_one.at[part, half],
                    w_sem.at[2 * part + half],
                )
                for part in range(2) for half in range(2)
            ]
        copies = []
        for part in range(2):
            for half in range(2):
                copies.append(pltpu.make_async_copy(
                    w2_hbm.at[part, pl.ds(0, 4), pl.ds(half * HALF, HALF)],
                    wv_two.at[part, pl.ds(4 * half, 4)], w_sem.at[len(copies)],
                ))
            copies.append(pltpu.make_async_copy(
                w2_hbm.at[part, 4, pl.ds(0, HALF)], wv_two.at[part, 8], w_sem.at[len(copies)],
            ))
            copies.append(pltpu.make_async_copy(
                w2_hbm.at[part, 4, pl.ds(HALF, HALF)], wv_two.at[part, 9], w_sem.at[len(copies)],
            ))
        for half in range(2):
            copies.append(pltpu.make_async_copy(
                w0_hbm.at[pl.ds(0, 6), pl.ds(half * HALF, HALF)],
                wv_zero.at[pl.ds(6 * half, 6)], w_sem.at[len(copies)],
            ))
        for half in range(2):
            copies.append(pltpu.make_async_copy(
                w0_hbm.at[6, pl.ds(half * HALF, HALF)], wv_zero.at[12 + half],
                w_sem.at[len(copies)],
            ))
        return copies

    for load in loads[1:]:
        load.wait()
    block = lax.broadcasted_iota(jnp.int32, (4, 128), 0)
    angle = ang_ref[...]
    alive = jnp.where(block < live_ref[0], env_ref[...], 0.0)
    edges[0:4] = src_ref[...].astype(F32)
    edges[4:8] = tgt_ref[...].astype(F32)
    edges[8:12] = alive
    edges[12:16] = alive * jnp.cos(angle)
    edges[16:20] = alive * jnp.sin(angle)
    edges[20:24] = alive * jnp.cos(2.0 * angle)
    edges[24:28] = alive * jnp.sin(2.0 * angle)
    edges[28:32] = jnp.zeros((4, 128), F32)

    for side in range(2):

        @pl.when(jnp.logical_not(has_help[side]))
        def _():
            for ref, width in zip(rx, WIDTH):
                for half in range(2):
                    ref[half, 2 * side] = jnp.zeros((ATOMS, width), BF16)

        @pl.when(jnp.logical_not(has_space[side]))
        def _():
            edges_in[side] = jnp.zeros((32, 128), F32)
            for ref, (rows, width) in zip(sums_in, SUMS):
                ref[side] = jnp.zeros((rows, width), BF16)

    loads[0].wait()
    for ref, order in zip(rx, PACK):
        for pair in range(len(order) // 2):
            ref[c, 1, :, pl.ds(128 * pair, 128)] = jnp.concatenate(
                [xv[order[2 * pair]], xv[order[2 * pair + 1]]], axis=1
            )

    expected = 1
    for side in range(2):
        expected = expected + 2 * has_help[side].astype(jnp.int32) + has_space[side].astype(jnp.int32)
    pl.semaphore_wait(barrier, expected)

    def edge_copy(side):
        return pltpu.make_async_remote_copy(
            src_ref=edges, dst_ref=edges_in.at[1 - side],
            send_sem=edge_send.at[side], recv_sem=edge_recv.at[1 - side],
            device_id=(s + 2 * side - 1, h, c), device_id_type=MESH,
        )

    def halo_copy(plane, side):
        return pltpu.make_async_remote_copy(
            src_ref=rx[plane].at[c, 1], dst_ref=rx[plane].at[c, 2 - 2 * side],
            send_sem=halo_send.at[plane, 2 * side], recv_sem=halo_recv.at[plane, c, 2 - 2 * side],
            device_id=(s, h + 2 * side - 1, min(plane, 1)), device_id_type=MESH,
        )

    def pair_copy(plane):
        return pltpu.make_async_remote_copy(
            src_ref=rx[plane].at[c, 1], dst_ref=rx[plane].at[c, 1],
            send_sem=halo_send.at[plane, 1], recv_sem=halo_recv.at[plane, c, 1],
            device_id=partner, device_id_type=MESH,
        )

    def sum_copy(plane, side):
        return pltpu.make_async_remote_copy(
            src_ref=tx[plane].at[side], dst_ref=sums_in[plane].at[1 - side],
            send_sem=sum_send.at[plane, side], recv_sem=sum_recv.at[plane, 1 - side],
            device_id=(s + 2 * side - 1, h, c), device_id_type=MESH,
        )

    def out_copy(plane):
        at = pl.ds(*OUT_AT[plane])
        return pltpu.make_async_remote_copy(
            src_ref=give.at[at], dst_ref=out_ref.at[at],
            send_sem=out_send.at[plane], recv_sem=out_recv.at[plane],
            device_id=partner, device_id_type=MESH,
        )

    def arrived(dst, sem):
        pltpu.make_async_copy(dst, dst, sem).wait()

    for side in range(2):

        @pl.when(has_space[side])
        def _():
            edge_copy(side).start()

    for plane in range(3):
        for side in range(2):

            @pl.when(has_help[side])
            def _():
                halo_copy(plane, side).start()

        @pl.when(c != min(plane, 1))
        def _():
            pair_copy(plane).start()

    ids_row = lax.broadcasted_iota(jnp.int32, (ROW, 128), 0).astype(F32)
    ids_atom = lax.broadcasted_iota(jnp.int32, (ATOMS, 128), 0).astype(F32)

    def gathering(which, picks):
        held = edges if which == 1 else edges_in.at[which // 2]
        first = float(ROW * (2 - which))
        left, right = [], []
        for b in range(4):
            source = held[b:b + 1] - first
            target = held[4 + b:5 + b] == ids_atom
            right.append(jnp.where(source == ids_row, 1.0, 0.0).astype(BF16))
            left.append(jnp.concatenate(
                [jnp.where(target, held[pick + b:pick + b + 1], 0.0) for pick in picks], axis=0
            ).astype(BF16))
        return lax.dot_general(
            jnp.concatenate(left, axis=1), jnp.concatenate(right, axis=1),
            (((1,), (1,)), ((), ())), preferred_element_type=F32,
        ).astype(BF16)

    def all_gatherings(picks):
        middle = gathering(1, picks)
        for side in range(2):

            @pl.when(has_space[side])
            def _():
                arrived(edges_in.at[side], edge_recv.at[side])

        return [gathering(0, picks), middle, gathering(2, picks)]

    def wait_halo(plane, own):
        for half in range(2):
            for side in range(2):

                @pl.when(has_help[side])
                def _():
                    arrived(rx[plane].at[half, 2 * side], halo_recv.at[plane, half, 2 * side])

        arrived(rx[plane].at[1 - own, 1], halo_recv.at[plane, 1 - own, 1])

    def send_sums(plane):
        for side in range(2):

            @pl.when(has_space[side])
            def _():
                sum_copy(plane, side).start()

    def total(plane, own_part):
        for side in range(2):

            @pl.when(has_space[side])
            def _():
                arrived(sums_in[plane].at[side], sum_recv.at[plane, side])

        ref = sums_in[plane]
        return (own_part + ref[0].astype(F32) + ref[1].astype(F32)).astype(BF16)

    def finish(plane, own, pieces):
        row = OUT_AT[plane][0]
        for piece in pieces:
            rounded = piece.astype(BF16)
            for degree in range(piece.shape[1] // 128):
                lower = rounded[:, 128 * degree:128 * degree + HALF]
                upper = rounded[:, 128 * degree + HALF:128 * degree + 128]
                out_ref[row] = (lower, upper)[own]
                give[row] = (upper, lower)[own]
                row += 1
        out_copy(plane).start()

    def by_lane(a, b):
        low = lax.broadcasted_iota(jnp.int32, a.shape, 1) < HALF
        return (
            jnp.where(low, a, pltpu.roll(b, HALF, 1)),
            jnp.where(low, pltpu.roll(a, HALF, 1), b),
        )

    def rotated_mix(lhs, real, imag):
        by_real, by_imag = dot(lhs, real), dot(lhs, imag)
        return [by_real[:ATOMS] - by_imag[ATOMS:], by_imag[:ATOMS] + by_real[ATOMS:]]

    @pl.when(c == 0)
    def _():
        copies = weight_copies(0)
        for copy in copies:
            copy.start()
        turn = jnp.concatenate(all_gatherings((12, 16)), axis=0)
        wait_halo(0, 0)
        parts = [dot(turn, rx_one[half].reshape(ROW, 768)) for half in range(2)]
        own_sum = None
        for which in range(3):
            at = 2 * ATOMS * which
            plus, minus = [], []
            for part in parts:
                by_cos, by_sin = part[at:at + ATOMS], part[at + ATOMS:at + 2 * ATOMS]
                plus.append(by_cos[:, :384] + by_sin[:, 384:])
                minus.append(by_cos[:, 384:] - by_sin[:, :384])
            both = jnp.concatenate(
                [jnp.concatenate(plus, axis=1), jnp.concatenate(minus, axis=1)], axis=0
            )
            if which == 1:
                own_sum = both
            else:
                tx_one[which // 2] = both.astype(BF16)
        send_sums(0)
        for copy in copies:
            copy.wait()
        summed = total(0, own_sum)
        finish(0, 0, rotated_mix(
            summed, wv_one[0].reshape(768, 768), wv_one[1].reshape(768, 768)
        ))
        out_copy(0).wait_send()
        for plane in (1, 2):
            at = pl.ds(*OUT_AT[plane])
            arrived(out_ref.at[at], out_recv.at[plane])
        for side in range(2):

            @pl.when(has_space[side])
            def _():
                sum_copy(0, side).wait_send()

        for plane in (1, 2):
            pair_copy(plane).wait_send()

    @pl.when(c == 1)
    def _():
        copies = weight_copies(1)
        for copy in copies:
            copy.start()
        full = all_gatherings((20, 24, 8))
        turn = jnp.concatenate([each[:2 * ATOMS] for each in full], axis=0)
        flat = jnp.concatenate([each[2 * ATOMS:] for each in full], axis=0)
        wait_halo(1, 1)
        parts = [dot(turn, rx_two[half].reshape(ROW, 640)) for half in range(2)]
        own_two = None
        for which in range(3):
            at = 2 * ATOMS * which
            plus, minus, tails = [], [], []
            low = lax.broadcasted_iota(jnp.int32, (ATOMS, 128), 1) < HALF
            for part in parts:
                by_cos, by_sin = part[at:at + ATOMS], part[at + ATOMS:at + 2 * ATOMS]
                plus.append(by_cos[:, :256] + by_sin[:, 256:512])
                minus.append(by_cos[:, 256:512] - by_sin[:, :256])
                crossed = pltpu.roll(by_sin[:, 512:], HALF, 1)
                tails.append(by_cos[:, 512:] + jnp.where(low, crossed, -crossed))
            plus_tail, minus_tail = by_lane(*tails)
            both = jnp.concatenate([
                jnp.concatenate(plus + [plus_tail], axis=1),
                jnp.concatenate(minus + [minus_tail], axis=1),
            ], axis=0)
            if which == 1:
                own_two = both
            else:
                tx_two[which // 2] = both.astype(BF16)
        send_sums(1)
        wait_halo(2, 1)
        parts = [dot(flat, rx_zero[half].reshape(ROW, 512)) for half in range(2)]
        own_zero = None
        for which in range(3):
            at = ATOMS * which
            one, two = parts[0][at:at + ATOMS], parts[1][at:at + ATOMS]
            tail, _unused = by_lane(one[:, 384:], two[:, 384:])
            whole = jnp.concatenate([one[:, :384], two[:, :384], tail], axis=1)
            if which == 1:
                own_zero = whole
            else:
                tx_zero[which // 2] = whole.astype(BF16)
        send_sums(2)
        for copy in copies:
            copy.wait()
        summed = total(1, own_two)
        finish(1, 1, rotated_mix(
            summed, wv_two[0].reshape(640, 640), wv_two[1].reshape(640, 640)
        ))
        summed = total(2, own_zero)
        finish(2, 1, [dot(summed, wv_zero[...].reshape(896, 896))])
        for plane in (1, 2):
            out_copy(plane).wait_send()
        arrived(out_ref.at[pl.ds(*OUT_AT[0])], out_recv.at[0])
        for plane in (1, 2):
            for side in range(2):

                @pl.when(has_space[side])
                def _():
                    sum_copy(plane, side).wait_send()

        pair_copy(0).wait_send()

    for side in range(2):

        @pl.when(has_space[side])
        def _():
            edge_copy(side).wait_send()

        @pl.when(has_help[side])
        def _():
            for plane in range(3):
                halo_copy(plane, side).wait_send()


def solution(mesh):
    n_space, n_help = mesh.shape["space"], mesh.shape["help"]

    def shards(node_feats, source_index, target_index, edge_angle, edge_envelope, live_blocks,
               w_zero, w_one, w_two):
        feats = jnp.transpose(node_feats, (1, 0, 2))
        anywhere = pl.BlockSpec(memory_space=pltpu.HBM)
        in_vmem = pl.BlockSpec(memory_space=pltpu.VMEM)
        dma = pltpu.SemaphoreType.DMA
        out = pl.pallas_call(
            functools.partial(kernel, n_space, n_help),
            out_shape=jax.ShapeDtypeStruct((29, ATOMS, HALF), BF16),
            in_specs=[anywhere] * 9,
            out_specs=in_vmem,
            scratch_shapes=[
                pltpu.VMEM((4, 128), jnp.int32), pltpu.VMEM((4, 128), jnp.int32),
                pltpu.VMEM((4, 128), F32), pltpu.VMEM((4, 128), F32),
                pltpu.SMEM((1,), jnp.int32),
                pltpu.VMEM(feats.shape, BF16),
                *[pltpu.VMEM((2, 3, ATOMS, width), BF16) for width in WIDTH],
                pltpu.VMEM((32, 128), F32),
                pltpu.VMEM((2, 32, 128), F32),
                *[pltpu.VMEM((2, *shape), BF16) for shape in SUMS],
                *[pltpu.VMEM((2, *shape), BF16) for shape in SUMS],
                pltpu.VMEM((2, 2, 6, HALF, 768), BF16),
                pltpu.VMEM((2, 10, HALF, 640), BF16),
                pltpu.VMEM((14, HALF, 896), BF16),
                pltpu.VMEM((29, ATOMS, HALF), BF16),
                dma((6,)), dma((12,)), dma((3, 3)), dma((3, 2, 3)), dma((2,)), dma((2,)),
                dma((3, 2)), dma((3, 2)), dma((3,)), dma((3,)),
            ],
            compiler_params=pltpu.CompilerParams(
                collective_id=0, has_side_effects=True, vmem_limit_bytes=63 * 1024 * 1024
            ),
            cost_estimate=pl.CostEstimate(
                flops=2 * 64 * 3 * 1024 * 1024, bytes_accessed=8 * 1024 * 1024, transcendentals=2048
            ),
            name="edge_mix",
        )(feats, source_index, target_index, edge_angle, edge_envelope, live_blocks,
          w_zero, w_one, w_two)
        return jnp.transpose(out, (1, 0, 2))

    return jax.shard_map(
        shards,
        mesh=mesh,
        in_specs=(
            P(("space", "help"), None, "chan"),
            P(("space", "help"), None),
            P(("space", "help"), None),
            P(("space", "help"), None),
            P(("space", "help"), None),
            P(("space", "help")),
            P(), P(), P(),
        ),
        out_specs=P(("space", "help"), None, "chan"),
        check_vma=False,
    )
```

time: 198 us -> 24.5 us (0.12)
  waiting for transfers between devices: 144 us -> 0 us
  Pallas kernels: 0 us -> 22.1 us
  local copies, waits for them, and re-layouts: 21.4 us -> 1.65 us
  starting transfers between devices: 13.1 us -> 0 us
  between operations: 13.5 us -> 0.66 us
  other arithmetic: 3.6 us -> 0 us
    unnamed x2 -> x0, waiting for transfers between devices: 139 us -> none
    pallas_call x0 -> x1, Pallas kernels: none -> 22.1 us  [shards(): pl.pallas_call(functools.partial(kernel, n_space, n_help), out_shape=jax....]
    ppermute x4 -> x0, starting transfers between devices: 13 us -> none  [the longest x2 10.2 us: with_halo(): lax.ppermute(tail, axis, [(i, (i + 1) % count) for i in range(ends)])]
    unnamed x24 -> x1, local copies, waits for them, and re-layouts: 9.52 us -> 1.65 us
    ppermute x4 -> x0, waiting for transfers between devices: 5.19 us -> none  [the longest x2 3.71 us: with_halo(): lax.ppermute(head, axis, [((i + 1) % count, i) for i in range(ends)])]
    slice x2 -> x0, local copies, waits for them, and re-layouts: 4.17 us -> none  [shards(): raw_weights = (w_zero, w_one[0], w_one[1], w_two[0], w_two[1])]
    dynamic_slice x3 -> x0, local copies, waits for them, and re-layouts: 2.87 us -> none  [input_rows(): picked = lax.dynamic_slice_in_dim(weight, chan_start, half_width, 1)]
    concatenate x2 -> x0, other arithmetic: 2.82 us -> none  [with_halo(): jnp.concatenate([lax.ppermute(tail, axis, [(i, (i + 1) % count) for i in...]
  transfers between devices with their start and end apart: 5 -> 0, of which waited for: 3 -> 0; matrix products, arithmetic and copies ran while one was open for 4% -> 0% of each run, Pallas kernels for 0% -> 0%
where the time goes in v1:
time: 24.5 us; the launch traced here: 24.4 us
  Pallas kernels  22.1 us (90%)
  local copies, waits for them, and re-layouts  1.65 us (7%)
  between operations  0.66 us (3%)
    pallas_call x1, Pallas kernels, shards(): pl.pallas_call(functools.partial(kernel, n_space, n_help), out_shape=jax....  22.1 us
    unnamed x1, local copies, waits for them, and re-layouts  1.65 us

profile of v1, /device:TPU:1, one launch (start us, length us, event | category | flops | bytes accessed | tf_op | source)
XLA Modules:
  0.0 24.4 jit_solution(9976539018664008562)
XLA Ops:
  0.7 22.1 %edge_mix.1 = bf16[29,32,64]{2,1,0:T(8,128)(2,1)} custom-call(bf16[49,32,64]{2,1,0:T(8,128)(2,1)} %bitcast.3, s32[4,128]{1,0:T(4,128)} %src_hbm.1, s32[4,128]{1,0:T(4,128)} %tgt_hbm.1, f32[4,128]{1,0:T(4,128)} %ang_hbm.1, f32[4,128]{1,0:T(4,128)} %env_hbm.1, s32[1]{0:T(128)S(6)} %copy.11.live_hbm, bf16[7,128,896]{2,1,0:T(8,128)(2,1)} %w0_hbm.1, ...), custom_call_target="tpu_custom_call" | custom-call | flops 402653184 | bytes 8388608 | tf_op jit(solution)/shard_map/edge_mix/pallas_call | solution.py:418
  22.7 1.6 %copy.12 = bf16[32,29,64]{2,0,1:T(8,128)(2,1)} copy(bf16[32,29,64]{2,0,1:T(8,128)(2,1)} %bitcast.2) | data formatting | bytes 237568

commit v2 on v0

v2 whole, which is shorter than its diff:
```python
import functools

import jax
import jax.numpy as jnp
from jax import lax
from jax.experimental import pallas as pl
from jax.experimental.pallas import tpu as pltpu
from jax.sharding import PartitionSpec as P

MESH = pl.DeviceIdType.MESH
F32, BF16 = jnp.float32, jnp.bfloat16
ATOMS = 32
HALF = 64
ROW = 3 * ATOMS

PLUS_ONE = [l * l + l + 1 for l in range(1, 7)]
MINUS_ONE = [l * l + l - 1 for l in range(1, 7)]
PLUS_TWO = [l * l + l + 2 for l in range(2, 7)]
MINUS_TWO = [l * l + l - 2 for l in range(2, 7)]
ZERO = [l * l + l for l in range(7)]
PACK = (
    PLUS_ONE + MINUS_ONE,
    PLUS_TWO[:4] + MINUS_TWO[:4] + [PLUS_TWO[4], MINUS_TWO[4]],
    ZERO + ZERO[-1:],
)
WIDTH = tuple(HALF * len(order) for order in PACK)
RUNS = [(0, 4)] + [(l * l + l - 2, 5) for l in range(2, 7)]
OUT_AT = ((7, 12), (19, 10), (0, 7))
GIVEN = (768, 640, 512)
COS_ONE, SIN_ONE, SOURCE, TARGET, COS_TWO, SIN_TWO, PLAIN = range(0, 28, 4)
EDGE_ROWS = (None, (0, 32))
FIRST = (0, 0, 0)


def dot(a, b):
    return jnp.dot(a, b, preferred_element_type=F32)


def kernel(
    n_space, n_help,
    x_hbm, src_hbm, tgt_hbm, ang_hbm, env_hbm, live_hbm, w0_hbm, w1_hbm, w2_hbm,
    out_ref,
    src_ref, tgt_ref, ang_ref, env_ref, live_ref, xv, rx_one, rx_two, rx_zero, edges, edges_in,
    tx_one, tx_two, tx_zero, in_one, in_two, in_zero,
    wv_one, wv_two, wv_zero, give_one, give_two, give_zero, take_one, take_two, take_zero,
    x_sem, in_sem, w_sem, halo_send, halo_recv, edge_send, edge_recv,
    sum_send, sum_recv, out_send, out_recv,
):
    s, h, c = lax.axis_index("space"), lax.axis_index("help"), lax.axis_index("chan")
    has = ((h > 0, h < n_help - 1), (s > 0, s < n_space - 1))
    rx = (rx_one, rx_two, rx_zero)
    tx = (tx_one, tx_two, tx_zero)
    sums_in = (in_one, in_two, in_zero)
    give = (give_one, give_two, give_zero)
    take = (take_one, take_two, take_zero)
    partner = (s, h, 1 - c)

    def neighbour(axis, side):
        step = 2 * side - 1
        return (s, h + step, c) if axis == 0 else (s + step, h, c)

    barrier = pltpu.get_barrier_semaphore()

    def greet(device):
        pl.semaphore_signal(barrier, inc=1, device_id=device, device_id_type=MESH)

    x_loads = [
        pltpu.make_async_copy(x_hbm.at[pl.ds(*run)], xv.at[pl.ds(*run)], x_sem.at[at])
        for at, run in enumerate(RUNS)
    ]
    loads = [
        pltpu.make_async_copy(source, held, in_sem.at[at])
        for at, (source, held) in enumerate((
            (src_hbm, src_ref), (tgt_hbm, tgt_ref), (ang_hbm, ang_ref),
            (env_hbm, env_ref), (live_hbm, live_ref),
        ))
    ]
    mine = pl.ds(pl.multiple_of(c * HALF, HALF), HALF)
    weights = [
        pltpu.make_async_copy(w1_hbm.at[:, :, mine], wv_one, w_sem.at[0]),
        pltpu.make_async_copy(w2_hbm.at[:, :, mine], wv_two, w_sem.at[1]),
        pltpu.make_async_copy(w0_hbm.at[:, mine], wv_zero, w_sem.at[2]),
    ]
    for load in x_loads:
        load.start()

    expected = 1
    for axis in range(2):
        for side in range(2):
            expected = expected + has[axis][side].astype(jnp.int32)

            @pl.when(has[axis][side])
            def _():
                greet(neighbour(axis, side))

    greet(partner)

    for load in loads:
        load.start()

    for axis in range(2):
        for side in range(2):

            @pl.when(jnp.logical_not(has[axis][side]))
            def _():
                edges_in[2 * axis + side] = jnp.zeros((32, 128), F32)
                for plane in range(3):
                    if FIRST[plane] == axis:
                        rx[plane][2 * side] = jnp.zeros((ATOMS, WIDTH[plane]), BF16)
                    else:
                        sums_in[plane][side] = jnp.zeros((ATOMS, WIDTH[plane]), BF16)

    def halo_copy(plane, side):
        return pltpu.make_async_remote_copy(
            src_ref=rx[plane].at[1], dst_ref=rx[plane].at[2 - 2 * side],
            send_sem=halo_send.at[plane, side], recv_sem=halo_recv.at[plane, 1 - side],
            device_id=neighbour(FIRST[plane], side), device_id_type=MESH,
        )

    def edge_copy(axis, side):
        rows = pl.ds(*EDGE_ROWS[axis])
        return pltpu.make_async_remote_copy(
            src_ref=edges.at[rows], dst_ref=edges_in.at[2 * axis + 1 - side, rows],
            send_sem=edge_send.at[axis, side], recv_sem=edge_recv.at[axis, 1 - side],
            device_id=neighbour(axis, side), device_id_type=MESH,
        )

    def sum_copy(plane, side):
        return pltpu.make_async_remote_copy(
            src_ref=tx[plane].at[side], dst_ref=sums_in[plane].at[1 - side],
            send_sem=sum_send.at[plane, side], recv_sem=sum_recv.at[plane, 1 - side],
            device_id=neighbour(1 - FIRST[plane], side), device_id_type=MESH,
        )

    def out_copy(plane):
        return pltpu.make_async_remote_copy(
            src_ref=give[plane], dst_ref=take[plane],
            send_sem=out_send.at[plane], recv_sem=out_recv.at[plane],
            device_id=partner, device_id_type=MESH,
        )

    for load in loads:
        load.wait()
    block = lax.broadcasted_iota(jnp.int32, (4, 128), 0)
    angle = ang_ref[...]
    alive = jnp.where(block < live_ref[0], env_ref[...], 0.0)
    for row, value in (
        (COS_ONE, alive * jnp.cos(angle)), (SIN_ONE, alive * jnp.sin(angle)),
        (SOURCE, src_ref[...].astype(F32)), (TARGET, tgt_ref[...].astype(F32)),
        (COS_TWO, alive * jnp.cos(2.0 * angle)), (SIN_TWO, alive * jnp.sin(2.0 * angle)),
        (PLAIN, alive), (PLAIN + 4, jnp.zeros((4, 128), F32)),
    ):
        edges[row:row + 4] = value
    for load in x_loads:
        load.wait()
    for plane, (ref, order) in enumerate(zip(rx, PACK)):
        for pair in range(len(order) // 2):
            ref[1, :, pl.ds(128 * pair, 128)] = jnp.concatenate(
                [xv[order[2 * pair]], xv[order[2 * pair + 1]]], axis=1
            )
        if plane == 0:
            pl.semaphore_wait(barrier, expected)
            for axis in (1,):
                for side in range(2):

                    @pl.when(has[axis][side])
                    def _():
                        edge_copy(axis, side).start()
        for side in range(2):

            @pl.when(has[FIRST[plane]][side])
            def _():
                halo_copy(plane, side).start()

    for load in weights:
        load.start()

    line = lax.broadcasted_iota(jnp.int32, (ROW, 128), 0)
    along_help = line.astype(F32)
    along_space = (line + 2 * ATOMS * (line // ATOMS)).astype(F32)
    ids_atom = lax.broadcasted_iota(jnp.int32, (ATOMS, 128), 0).astype(F32)

    def gathering(axis, which, picks):
        held = edges if which == 1 else edges_in.at[2 * (1 - axis) + which // 2]
        names = along_help if axis == 0 else along_space
        first = float((2 - which) * (ROW if axis == 0 else ATOMS))
        left, right = [], []
        for b in range(4):
            source = held[SOURCE + b:SOURCE + b + 1] - first
            target = held[TARGET + b:TARGET + b + 1] == ids_atom
            right.append(jnp.where(source == names, 1.0, 0.0).astype(BF16))
            left.append(jnp.concatenate(
                [jnp.where(target, held[at + b:at + b + 1], 0.0) for at in picks], axis=0
            ).astype(BF16))
        return lax.dot_general(
            jnp.concatenate(left, axis=1), jnp.concatenate(right, axis=1),
            (((1,), (1,)), ((), ())), preferred_element_type=F32,
        ).astype(BF16)

    picks = (COS_ONE, SIN_ONE, COS_TWO, SIN_TWO, PLAIN)
    middle = gathering(0, 1, picks)
    for side in range(2):

        @pl.when(has[1][side])
        def _():
            edge_copy(1, 1 - side).wait_recv()

    full = [gathering(0, 0, picks), middle, gathering(0, 2, picks)]
    lhs = [
        jnp.concatenate([each[first:first + rows] for each in full], axis=0)
        for first, rows in ((0, 2 * ATOMS), (2 * ATOMS, 2 * ATOMS), (4 * ATOMS, ATOMS))
    ]
    low = lax.broadcasted_iota(jnp.int32, (ATOMS, 128), 1) < HALF

    def turned(plane, part):
        if plane == 2:
            return part
        by_cos, by_sin = part[:ATOMS], part[ATOMS:]
        if plane == 0:
            return jnp.concatenate([
                by_cos[:, :384] + by_sin[:, 384:], by_cos[:, 384:] - by_sin[:, :384]
            ], axis=1)
        crossed = pltpu.roll(by_sin[:, 512:], HALF, 1)
        return jnp.concatenate([
            by_cos[:, :256] + by_sin[:, 256:512],
            by_cos[:, 256:512] - by_sin[:, :256],
            by_cos[:, 512:] + jnp.where(low, crossed, -crossed),
        ], axis=1)

    own = []
    for plane in range(3):
        for side in range(2):

            @pl.when(has[FIRST[plane]][side])
            def _():
                halo_copy(plane, 1 - side).wait_recv()

        part = dot(lhs[plane], rx[plane][...].reshape(ROW, WIDTH[plane]))
        rows = part.shape[0] // 3
        for side in range(2):
            tx[plane][side] = turned(plane, part[2 * side * rows:(2 * side + 1) * rows]).astype(BF16)

            @pl.when(has[1 - FIRST[plane]][side])
            def _():
                sum_copy(plane, side).start()

        own.append(turned(plane, part[rows:2 * rows]))

    for axis in range(2):
        for side in range(2):

            @pl.when(has[axis][side])
            def _():
                if axis == 1:
                    edge_copy(axis, side).wait_send()
                for plane in range(3):
                    if FIRST[plane] == axis:
                        halo_copy(plane, side).wait_send()

    for load in weights:
        load.wait()

    def by_lane(a, b):
        return (
            jnp.where(low, a, pltpu.roll(b, HALF, 1)),
            jnp.where(low, pltpu.roll(a, HALF, 1), b),
        )

    def rotated_mix(sums, real, imag):
        by_real, by_imag = dot(sums, real), dot(sums, imag)
        return [by_real[:ATOMS] - by_imag[ATOMS:], by_imag[:ATOMS] + by_real[ATOMS:]]

    first_core = c == 0
    kept = []
    for plane in range(3):
        for side in range(2):

            @pl.when(has[1 - FIRST[plane]][side])
            def _():
                sum_copy(plane, 1 - side).wait_recv()

        y = own[plane] + sums_in[plane][0].astype(F32) + sums_in[plane][1].astype(F32)
        if plane == 0:
            mixed = rotated_mix(
                jnp.concatenate([y[:, :384], y[:, 384:]], axis=0).astype(BF16),
                wv_one[0].reshape(384, 768), wv_one[1].reshape(384, 768),
            )
        elif plane == 1:
            tail = y[:, 512:]
            mixed = rotated_mix(
                jnp.concatenate([
                    jnp.concatenate([y[:, :256], tail], axis=1),
                    jnp.concatenate([y[:, 256:512], pltpu.roll(tail, HALF, 1)], axis=1),
                ], axis=0).astype(BF16)[:, :320],
                wv_two[0].reshape(320, 640), wv_two[1].reshape(320, 640),
            )
        else:
            mixed = [dot(y[:, :448].astype(BF16), wv_zero[...].reshape(448, 896))]
        blocks = [
            piece[:, 128 * degree:128 * degree + 128]
            for piece in mixed for degree in range(piece.shape[1] // 128)
        ]
        keep = []
        for pair in range((len(blocks) + 1) // 2):
            lower, upper = by_lane(blocks[2 * pair], blocks[min(2 * pair + 1, len(blocks) - 1)])
            keep.append(jnp.where(first_core, lower, upper))
            give[plane][:, pl.ds(128 * pair, 128)] = jnp.where(first_core, upper, lower).astype(BF16)
        kept.append(keep)
        out_copy(plane).start()

    for plane in range(3):
        for side in range(2):

            @pl.when(has[1 - FIRST[plane]][side])
            def _():
                sum_copy(plane, side).wait_send()

    for plane in range(3):
        out_copy(plane).wait_recv()
        row, count = OUT_AT[plane]
        for pair, keep in enumerate(kept[plane]):
            whole = (keep + take[plane][:, pl.ds(128 * pair, 128)].astype(F32)).astype(BF16)
            out_ref[row + 2 * pair] = whole[:, :HALF]
            if 2 * pair + 1 < count:
                out_ref[row + 2 * pair + 1] = whole[:, HALF:]

    for plane in range(3):
        out_copy(plane).wait_send()


def solution(mesh):
    n_space, n_help = mesh.shape["space"], mesh.shape["help"]

    def shards(node_feats, source_index, target_index, edge_angle, edge_envelope, live_blocks,
               w_zero, w_one, w_two):
        feats = jnp.transpose(node_feats, (1, 0, 2))
        anywhere = pl.BlockSpec(memory_space=pltpu.HBM)
        in_vmem = pl.BlockSpec(memory_space=pltpu.VMEM)
        dma = pltpu.SemaphoreType.DMA
        out = pl.pallas_call(
            functools.partial(kernel, n_space, n_help),
            out_shape=pltpu.VMEM((29, ATOMS, HALF), BF16),
            in_specs=[anywhere] * 9,
            out_specs=in_vmem,
            scratch_shapes=[
                pltpu.VMEM((4, 128), jnp.int32), pltpu.VMEM((4, 128), jnp.int32),
                pltpu.VMEM((4, 128), F32), pltpu.VMEM((4, 128), F32),
                pltpu.SMEM((1,), jnp.int32),
                pltpu.VMEM(feats.shape, BF16),
                *[pltpu.VMEM((3, ATOMS, width), BF16) for width in WIDTH],
                pltpu.VMEM((32, 128), F32),
                pltpu.VMEM((4, 32, 128), F32),
                *[pltpu.VMEM((2, ATOMS, width), BF16) for width in WIDTH + WIDTH],
                pltpu.VMEM((2, 6, HALF, 768), BF16),
                pltpu.VMEM((2, 5, HALF, 640), BF16),
                pltpu.VMEM((7, HALF, 896), BF16),
                *[pltpu.VMEM((ATOMS, width), BF16) for width in GIVEN + GIVEN],
                dma((6,)), dma((5,)), dma((3,)), dma((3, 2)), dma((3, 2)), dma((2, 2)), dma((2, 2)),
                dma((3, 2)), dma((3, 2)), dma((3,)), dma((3,)),
            ],
            compiler_params=pltpu.CompilerParams(
                collective_id=0, has_side_effects=True, vmem_limit_bytes=60 * 1024 * 1024
            ),
            cost_estimate=pl.CostEstimate(
                flops=2 * 64 * 3 * 1024 * 1024, bytes_accessed=8 * 1024 * 1024, transcendentals=2048
            ),
            name="edge_mix",
        )(feats, source_index, target_index, edge_angle, edge_envelope, live_blocks,
          w_zero, w_one, w_two)
        return jnp.transpose(out, (1, 0, 2))

    return jax.shard_map(
        shards,
        mesh=mesh,
        in_specs=(
            P(("space", "help"), None, "chan"),
            P(("space", "help"), None),
            P(("space", "help"), None),
            P(("space", "help"), None),
            P(("space", "help"), None),
            P(("space", "help")),
            P(), P(), P(),
        ),
        out_specs=P(("space", "help"), None, "chan"),
        check_vma=False,
    )
```

time: 198 us -> 22.7 us (0.11)
  waiting for transfers between devices: 144 us -> 0 us
  Pallas kernels: 0 us -> 21.2 us
  local copies, waits for them, and re-layouts: 21.4 us -> 0.69 us
  starting transfers between devices: 13.1 us -> 0 us
  between operations: 13.5 us -> 0.66 us
  other arithmetic: 3.6 us -> 0 us
    unnamed x2 -> x0, waiting for transfers between devices: 139 us -> none
    pallas_call x0 -> x1, Pallas kernels: none -> 21.2 us  [shards(): pl.pallas_call(functools.partial(kernel, n_space, n_help), out_shape=pltp...]
    ppermute x4 -> x0, starting transfers between devices: 13 us -> none  [the longest x2 10.2 us: with_halo(): lax.ppermute(tail, axis, [(i, (i + 1) % count) for i in range(ends)])]
    unnamed x24 -> x1, local copies, waits for them, and re-layouts: 9.52 us -> 0.69 us
    ppermute x4 -> x0, waiting for transfers between devices: 5.19 us -> none  [the longest x2 3.71 us: with_halo(): lax.ppermute(head, axis, [((i + 1) % count, i) for i in range(ends)])]
    slice x2 -> x0, local copies, waits for them, and re-layouts: 4.17 us -> none  [shards(): raw_weights = (w_zero, w_one[0], w_one[1], w_two[0], w_two[1])]
    dynamic_slice x3 -> x0, local copies, waits for them, and re-layouts: 2.87 us -> none  [input_rows(): picked = lax.dynamic_slice_in_dim(weight, chan_start, half_width, 1)]
    concatenate x2 -> x0, other arithmetic: 2.82 us -> none  [with_halo(): jnp.concatenate([lax.ppermute(tail, axis, [(i, (i + 1) % count) for i in...]
  transfers between devices with their start and end apart: 5 -> 0, of which waited for: 3 -> 0; matrix products, arithmetic and copies ran while one was open for 4% -> 0% of each run, Pallas kernels for 0% -> 0%
where the time goes in v2:
time: 22.7 us; the launch traced here: 22.5 us
  Pallas kernels  21.2 us (93%)
  local copies, waits for them, and re-layouts  0.69 us (3%)
  between operations  0.66 us (3%)
    pallas_call x1, Pallas kernels, shards(): pl.pallas_call(functools.partial(kernel, n_space, n_help), out_shape=pltp...  21.2 us
    unnamed x1, local copies, waits for them, and re-layouts  0.69 us

profile of v2, /device:TPU:1, one launch (start us, length us, event | category | flops | bytes accessed | tf_op | source)
XLA Modules:
  0.0 22.5 jit_solution(12841255841867690621)
XLA Ops:
  0.7 21.2 %edge_mix.1 = bf16[29,32,64]{2,1,0:T(8,128)(2,1)S(1)} custom-call(bf16[49,32,64]{2,1,0:T(8,128)(2,1)} %bitcast.3, s32[4,128]{1,0:T(4,128)} %src_hbm.1, s32[4,128]{1,0:T(4,128)} %tgt_hbm.1, f32[4,128]{1,0:T(4,128)} %ang_hbm.1, f32[4,128]{1,0:T(4,128)} %env_hbm.1, s32[1]{0:T(128)S(6)} %copy.12.live_hbm, bf16[7,128,896]{2,1,0:T(8,128)(2,1)} %w0_hbm.1, ...), custom_call_target="tpu_custom_call" | custom-call | flops 402653184 | bytes 8388608 | tf_op jit(solution)/shard_map/edge_mix/pallas_call | solution.py:340
  21.8 0.7 %copy.11 = bf16[32,29,64]{2,0,1:T(8,128)(2,1)} copy(bf16[32,29,64]{2,0,1:T(8,128)(2,1)S(1)} %bitcast.2) | data formatting | bytes 237568

commit v3 on v2

--- a/solution.py
+++ b/solution.py
@@ -27,8 +27,7 @@
 RUNS = [(0, 4)] + [(l * l + l - 2, 5) for l in range(2, 7)]
 OUT_AT = ((7, 12), (19, 10), (0, 7))
 GIVEN = (768, 640, 512)
-COS_ONE, SIN_ONE, SOURCE, TARGET, COS_TWO, SIN_TWO, PLAIN = range(0, 28, 4)
-EDGE_ROWS = (None, (0, 32))
+COS_ONE, SIN_ONE, COS_TWO, SIN_TWO, PLAIN = range(0, 20, 4)
 FIRST = (0, 0, 0)
 
 
@@ -38,9 +37,9 @@
 
 def kernel(
     n_space, n_help,
-    x_hbm, src_hbm, tgt_hbm, ang_hbm, env_hbm, live_hbm, w0_hbm, w1_hbm, w2_hbm,
+    x_hbm, src_hbm, tgt_hbm, ang_hbm, env_hbm, live_ref, w0_hbm, w1_hbm, w2_hbm,
     out_ref,
-    src_ref, tgt_ref, ang_ref, env_ref, live_ref, xv, rx_one, rx_two, rx_zero, edges, edges_in,
+    src_ref, tgt_ref, ang_ref, env_ref, live_at, xv, rx_one, rx_two, rx_zero, edges,
     tx_one, tx_two, tx_zero, in_one, in_two, in_zero,
     wv_one, wv_two, wv_zero, give_one, give_two, give_zero, take_one, take_two, take_zero,
     x_sem, in_sem, w_sem, halo_send, halo_recv, edge_send, edge_recv,
@@ -68,12 +67,11 @@
         pltpu.make_async_copy(x_hbm.at[pl.ds(*run)], xv.at[pl.ds(*run)], x_sem.at[at])
         for at, run in enumerate(RUNS)
     ]
+    raw_hbm = (src_hbm, tgt_hbm, ang_hbm, env_hbm)
+    raw = (src_ref, tgt_ref, ang_ref, env_ref, live_at)
     loads = [
-        pltpu.make_async_copy(source, held, in_sem.at[at])
-        for at, (source, held) in enumerate((
-            (src_hbm, src_ref), (tgt_hbm, tgt_ref), (ang_hbm, ang_ref),
-            (env_hbm, env_ref), (live_hbm, live_ref),
-        ))
+        pltpu.make_async_copy(source, held.at[1], in_sem.at[at])
+        for at, (source, held) in enumerate(zip(raw_hbm, raw))
     ]
     mine = pl.ds(pl.multiple_of(c * HALF, HALF), HALF)
     weights = [
@@ -98,12 +96,16 @@
     for load in loads:
         load.start()
 
+    live_at[1] = jnp.full((8, 128), live_ref[0], jnp.int32)
+
     for axis in range(2):
         for side in range(2):
 
             @pl.when(jnp.logical_not(has[axis][side]))
             def _():
-                edges_in[2 * axis + side] = jnp.zeros((32, 128), F32)
+                if axis == 1:
+                    for ref in raw:
+                        ref[2 * side] = jnp.zeros(ref.shape[1:], ref.dtype)
                 for plane in range(3):
                     if FIRST[plane] == axis:
                         rx[plane][2 * side] = jnp.zeros((ATOMS, WIDTH[plane]), BF16)
@@ -117,13 +119,15 @@
             device_id=neighbour(FIRST[plane], side), device_id_type=MESH,
         )
 
-    def edge_copy(axis, side):
-        rows = pl.ds(*EDGE_ROWS[axis])
-        return pltpu.make_async_remote_copy(
-            src_ref=edges.at[rows], dst_ref=edges_in.at[2 * axis + 1 - side, rows],
-            send_sem=edge_send.at[axis, side], recv_sem=edge_recv.at[axis, 1 - side],
-            device_id=neighbour(axis, side), device_id_type=MESH,
-        )
+    def edge_copies(side):
+        return [
+            pltpu.make_async_remote_copy(
+                src_ref=held.at[1] if at == 4 else raw_hbm[at], dst_ref=held.at[2 - 2 * side],
+                send_sem=edge_send.at[side, at], recv_sem=edge_recv.at[1 - side, at],
+                device_id=neighbour(1, side), device_id_type=MESH,
+            )
+            for at, held in enumerate(raw)
+        ]
 
     def sum_copy(plane, side):
         return pltpu.make_async_remote_copy(
@@ -139,18 +143,14 @@
             device_id=partner, device_id_type=MESH,
         )
 
-    for load in loads:
-        load.wait()
-    block = lax.broadcasted_iota(jnp.int32, (4, 128), 0)
-    angle = ang_ref[...]
-    alive = jnp.where(block < live_ref[0], env_ref[...], 0.0)
-    for row, value in (
-        (COS_ONE, alive * jnp.cos(angle)), (SIN_ONE, alive * jnp.sin(angle)),
-        (SOURCE, src_ref[...].astype(F32)), (TARGET, tgt_ref[...].astype(F32)),
-        (COS_TWO, alive * jnp.cos(2.0 * angle)), (SIN_TWO, alive * jnp.sin(2.0 * angle)),
-        (PLAIN, alive), (PLAIN + 4, jnp.zeros((4, 128), F32)),
-    ):
-        edges[row:row + 4] = value
+    pl.semaphore_wait(barrier, expected)
+    for side in range(2):
+
+        @pl.when(has[1][side])
+        def _():
+            for copy in edge_copies(side):
+                copy.start()
+
     for load in x_loads:
         load.wait()
     for plane, (ref, order) in enumerate(zip(rx, PACK)):
@@ -158,14 +158,6 @@
             ref[1, :, pl.ds(128 * pair, 128)] = jnp.concatenate(
                 [xv[order[2 * pair]], xv[order[2 * pair + 1]]], axis=1
             )
-        if plane == 0:
-            pl.semaphore_wait(barrier, expected)
-            for axis in (1,):
-                for side in range(2):
-
-                    @pl.when(has[axis][side])
-                    def _():
-                        edge_copy(axis, side).start()
         for side in range(2):
 
             @pl.when(has[FIRST[plane]][side])
@@ -175,37 +167,48 @@
     for load in weights:
         load.start()
 
-    line = lax.broadcasted_iota(jnp.int32, (ROW, 128), 0)
-    along_help = line.astype(F32)
-    along_space = (line + 2 * ATOMS * (line // ATOMS)).astype(F32)
-    ids_atom = lax.broadcasted_iota(jnp.int32, (ATOMS, 128), 0).astype(F32)
-
-    def gathering(axis, which, picks):
-        held = edges if which == 1 else edges_in.at[2 * (1 - axis) + which // 2]
-        names = along_help if axis == 0 else along_space
-        first = float((2 - which) * (ROW if axis == 0 else ATOMS))
+    ids_row = lax.broadcasted_iota(jnp.int32, (ROW, 128), 0)
+    ids_atom = lax.broadcasted_iota(jnp.int32, (ATOMS, 128), 0)
+    block = lax.broadcasted_iota(jnp.int32, (4, 128), 0)
+
+    def weigh(which):
+        angle = ang_ref[which]
+        alive = jnp.where(block < live_at[which, 0:4], env_ref[which], 0.0)
+        for row, value in (
+            (COS_ONE, alive * jnp.cos(angle)), (SIN_ONE, alive * jnp.sin(angle)),
+            (COS_TWO, alive * jnp.cos(2.0 * angle)), (SIN_TWO, alive * jnp.sin(2.0 * angle)),
+            (PLAIN, alive),
+        ):
+            edges[which, row:row + 4] = value
+
+    def gathering(which):
         left, right = [], []
         for b in range(4):
-            source = held[SOURCE + b:SOURCE + b + 1] - first
-            target = held[TARGET + b:TARGET + b + 1] == ids_atom
-            right.append(jnp.where(source == names, 1.0, 0.0).astype(BF16))
-            left.append(jnp.concatenate(
-                [jnp.where(target, held[at + b:at + b + 1], 0.0) for at in picks], axis=0
-            ).astype(BF16))
+            source = src_ref[which, b:b + 1] - ROW * (2 - which)
+            target = tgt_ref[which, b:b + 1] == ids_atom
+            right.append(jnp.where(source == ids_row, 1.0, 0.0).astype(BF16))
+            left.append(jnp.concatenate([
+                jnp.where(target, edges[which, at + b:at + b + 1], 0.0)
+                for at in (COS_ONE, SIN_ONE, COS_TWO, SIN_TWO, PLAIN)
+            ], axis=0).astype(BF16))
         return lax.dot_general(
             jnp.concatenate(left, axis=1), jnp.concatenate(right, axis=1),
             (((1,), (1,)), ((), ())), preferred_element_type=F32,
         ).astype(BF16)
 
-    picks = (COS_ONE, SIN_ONE, COS_TWO, SIN_TWO, PLAIN)
-    middle = gathering(0, 1, picks)
+    for load in loads:
+        load.wait()
+    weigh(1)
+    middle = gathering(1)
     for side in range(2):
 
         @pl.when(has[1][side])
         def _():
-            edge_copy(1, 1 - side).wait_recv()
-
-    full = [gathering(0, 0, picks), middle, gathering(0, 2, picks)]
+            for copy in edge_copies(1 - side):
+                copy.wait_recv()
+
+        weigh(2 * side)
+    full = [gathering(0), middle, gathering(2)]
     lhs = [
         jnp.concatenate([each[first:first + rows] for each in full], axis=0)
         for first, rows in ((0, 2 * ATOMS), (2 * ATOMS, 2 * ATOMS), (4 * ATOMS, ATOMS))
@@ -252,7 +255,8 @@
             @pl.when(has[axis][side])
             def _():
                 if axis == 1:
-                    edge_copy(axis, side).wait_send()
+                    for copy in edge_copies(side):
+                        copy.wait_send()
                 for plane in range(3):
                     if FIRST[plane] == axis:
                         halo_copy(plane, side).wait_send()
@@ -340,22 +344,20 @@
         out = pl.pallas_call(
             functools.partial(kernel, n_space, n_help),
             out_shape=pltpu.VMEM((29, ATOMS, HALF), BF16),
-            in_specs=[anywhere] * 9,
+            in_specs=[anywhere] * 5 + [pl.BlockSpec(memory_space=pltpu.SMEM)] + [anywhere] * 3,
             out_specs=in_vmem,
             scratch_shapes=[
-                pltpu.VMEM((4, 128), jnp.int32), pltpu.VMEM((4, 128), jnp.int32),
-                pltpu.VMEM((4, 128), F32), pltpu.VMEM((4, 128), F32),
-                pltpu.SMEM((1,), jnp.int32),
+                *[pltpu.VMEM((3, 4, 128), kind) for kind in (jnp.int32, jnp.int32, F32, F32)],
+                pltpu.VMEM((3, 8, 128), jnp.int32),
                 pltpu.VMEM(feats.shape, BF16),
                 *[pltpu.VMEM((3, ATOMS, width), BF16) for width in WIDTH],
-                pltpu.VMEM((32, 128), F32),
-                pltpu.VMEM((4, 32, 128), F32),
+                pltpu.VMEM((3, 24, 128), F32),
                 *[pltpu.VMEM((2, ATOMS, width), BF16) for width in WIDTH + WIDTH],
                 pltpu.VMEM((2, 6, HALF, 768), BF16),
                 pltpu.VMEM((2, 5, HALF, 640), BF16),
                 pltpu.VMEM((7, HALF, 896), BF16),
                 *[pltpu.VMEM((ATOMS, width), BF16) for width in GIVEN + GIVEN],
-                dma((6,)), dma((5,)), dma((3,)), dma((3, 2)), dma((3, 2)), dma((2, 2)), dma((2, 2)),
+                dma((6,)), dma((4,)), dma((3,)), dma((3, 2)), dma((3, 2)), dma((2, 5)), dma((2, 5)),
                 dma((3, 2)), dma((3, 2)), dma((3,)), dma((3,)),
             ],
             compiler_params=pltpu.CompilerParams(

time: 22.7 us -> 22.2 us (0.978)
  Pallas kernels: 21.2 us -> 20.7 us
    pallas_call x1, Pallas kernels: 21.2 us -> 20.7 us  [shards(): pl.pallas_call(functools.partial(kernel, n_space, n_help), out_shape=pltp...]
where the time goes in v3:
time: 22.2 us; the launch traced here: 22 us
  Pallas kernels  20.7 us (93%)
  local copies, waits for them, and re-layouts  0.69 us (3%)
  between operations  0.66 us (3%)
    pallas_call x1, Pallas kernels, shards(): pl.pallas_call(functools.partial(kernel, n_space, n_help), out_shape=pltp...  20.7 us
    unnamed x1, local copies, waits for them, and re-layouts  0.69 us

profile of v3, /device:TPU:1, one launch (start us, length us, event | category | flops | bytes accessed | tf_op | source)
XLA Modules:
  0.0 22.0 jit_solution(4004519578983045692)
XLA Ops:
  0.7 20.7 %edge_mix.1 = bf16[29,32,64]{2,1,0:T(8,128)(2,1)S(1)} custom-call(bf16[49,32,64]{2,1,0:T(8,128)(2,1)} %bitcast.3, s32[4,128]{1,0:T(4,128)} %src_hbm.1, s32[4,128]{1,0:T(4,128)} %tgt_hbm.1, f32[4,128]{1,0:T(4,128)} %ang_hbm.1, f32[4,128]{1,0:T(4,128)} %env_hbm.1, s32[1]{0:T(128)S(6)} %copy.12.live_ref, bf16[7,128,896]{2,1,0:T(8,128)(2,1)} %w0_hbm.1, ...), custom_call_target="tpu_custom_call" | custom-call | flops 402653184 | bytes 8388608 | tf_op jit(solution)/shard_map/edge_mix/pallas_call | solution.py:344
  21.3 0.7 %copy.11 = bf16[32,29,64]{2,0,1:T(8,128)(2,1)} copy(bf16[32,29,64]{2,0,1:T(8,128)(2,1)S(1)} %bitcast.2) | data formatting | bytes 237568

commit v4 on v3

--- a/solution.py
+++ b/solution.py
@@ -63,6 +63,16 @@
     def greet(device):
         pl.semaphore_signal(barrier, inc=1, device_id=device, device_id_type=MESH)
 
+    greet(partner)
+    expected = 1
+    for axis in (1, 0):
+        for side in (1, 0):
+            expected = expected + has[axis][side].astype(jnp.int32)
+
+            @pl.when(has[axis][side])
+            def _():
+                greet(neighbour(axis, side))
+
     x_loads = [
         pltpu.make_async_copy(x_hbm.at[pl.ds(*run)], xv.at[pl.ds(*run)], x_sem.at[at])
         for at, run in enumerate(RUNS)
@@ -79,38 +89,10 @@
         pltpu.make_async_copy(w2_hbm.at[:, :, mine], wv_two, w_sem.at[1]),
         pltpu.make_async_copy(w0_hbm.at[:, mine], wv_zero, w_sem.at[2]),
     ]
-    for load in x_loads:
+    for load in x_loads + loads:
         load.start()
 
-    expected = 1
-    for axis in range(2):
-        for side in range(2):
-            expected = expected + has[axis][side].astype(jnp.int32)
-
-            @pl.when(has[axis][side])
-            def _():
-                greet(neighbour(axis, side))
-
-    greet(partner)
-
-    for load in loads:
-        load.start()
-
     live_at[1] = jnp.full((8, 128), live_ref[0], jnp.int32)
-
-    for axis in range(2):
-        for side in range(2):
-
-            @pl.when(jnp.logical_not(has[axis][side]))
-            def _():
-                if axis == 1:
-                    for ref in raw:
-                        ref[2 * side] = jnp.zeros(ref.shape[1:], ref.dtype)
-                for plane in range(3):
-                    if FIRST[plane] == axis:
-                        rx[plane][2 * side] = jnp.zeros((ATOMS, WIDTH[plane]), BF16)
-                    else:
-                        sums_in[plane][side] = jnp.zeros((ATOMS, WIDTH[plane]), BF16)
 
     def halo_copy(plane, side):
         return pltpu.make_async_remote_copy(
@@ -167,16 +149,31 @@
     for load in weights:
         load.start()
 
+    for axis in range(2):
+        for side in range(2):
+
+            @pl.when(jnp.logical_not(has[axis][side]))
+            def _():
+                if axis == 1:
+                    for ref in raw:
+                        ref[2 * side] = jnp.zeros(ref.shape[1:], ref.dtype)
+                for plane in range(3):
+                    if FIRST[plane] == axis:
+                        rx[plane][2 * side] = jnp.zeros((ATOMS, WIDTH[plane]), BF16)
+                    else:
+                        sums_in[plane][side] = jnp.zeros((ATOMS, WIDTH[plane]), BF16)
+
     ids_row = lax.broadcasted_iota(jnp.int32, (ROW, 128), 0)
     ids_atom = lax.broadcasted_iota(jnp.int32, (ATOMS, 128), 0)
     block = lax.broadcasted_iota(jnp.int32, (4, 128), 0)
 
     def weigh(which):
         angle = ang_ref[which]
+        cos, sin = jnp.cos(angle), jnp.sin(angle)
         alive = jnp.where(block < live_at[which, 0:4], env_ref[which], 0.0)
         for row, value in (
-            (COS_ONE, alive * jnp.cos(angle)), (SIN_ONE, alive * jnp.sin(angle)),
-            (COS_TWO, alive * jnp.cos(2.0 * angle)), (SIN_TWO, alive * jnp.sin(2.0 * angle)),
+            (COS_ONE, alive * cos), (SIN_ONE, alive * sin),
+            (COS_TWO, alive * ((cos - sin) * (cos + sin))), (SIN_TWO, alive * (2.0 * cos * sin)),
             (PLAIN, alive),
         ):
             edges[which, row:row + 4] = value
@@ -200,7 +197,8 @@
         load.wait()
     weigh(1)
     middle = gathering(1)
-    for side in range(2):
+    gathered = [None, middle, None]
+    for side in (1, 0):
 
         @pl.when(has[1][side])
         def _():
@@ -208,9 +206,9 @@
                 copy.wait_recv()
 
         weigh(2 * side)
-    full = [gathering(0), middle, gathering(2)]
+        gathered[2 * side] = gathering(2 * side)
     lhs = [
-        jnp.concatenate([each[first:first + rows] for each in full], axis=0)
+        jnp.concatenate([each[first:first + rows] for each in gathered], axis=0)
         for first, rows in ((0, 2 * ATOMS), (2 * ATOMS, 2 * ATOMS), (4 * ATOMS, ATOMS))
     ]
     low = lax.broadcasted_iota(jnp.int32, (ATOMS, 128), 1) < HALF

time: 22.2 us -> 22.1 us (level)
  no operation moved by 1% of the time
where the time goes in v4:
time: 22.1 us; the launch traced here: 21.9 us
  Pallas kernels  20.5 us (93%)
  local copies, waits for them, and re-layouts  0.69 us (3%)
  between operations  0.66 us (3%)
    pallas_call x1, Pallas kernels, shards(): pl.pallas_call(functools.partial(kernel, n_space, n_help), out_shape=pltp...  20.5 us
    unnamed x1, local copies, waits for them, and re-layouts  0.69 us

profile of v4, /device:TPU:1, one launch (start us, length us, event | category | flops | bytes accessed | tf_op | source)
XLA Modules:
  0.0 21.9 jit_solution(1854961825519178870)
XLA Ops:
  0.7 20.5 %edge_mix.1 = bf16[29,32,64]{2,1,0:T(8,128)(2,1)S(1)} custom-call(bf16[49,32,64]{2,1,0:T(8,128)(2,1)} %bitcast.3, s32[4,128]{1,0:T(4,128)} %src_hbm.1, s32[4,128]{1,0:T(4,128)} %tgt_hbm.1, f32[4,128]{1,0:T(4,128)} %ang_hbm.1, f32[4,128]{1,0:T(4,128)} %env_hbm.1, s32[1]{0:T(128)S(6)} %copy.12.live_ref, bf16[7,128,896]{2,1,0:T(8,128)(2,1)} %w0_hbm.1, ...), custom_call_target="tpu_custom_call" | custom-call | flops 402653184 | bytes 8388608 | tf_op jit(solution)/shard_map/edge_mix/pallas_call | solution.py:342
  21.2 0.7 %copy.11 = bf16[32,29,64]{2,0,1:T(8,128)(2,1)} copy(bf16[32,29,64]{2,0,1:T(8,128)(2,1)S(1)} %bitcast.2) | data formatting | bytes 237568

commit v5 on v4

--- a/solution.py
+++ b/solution.py
@@ -39,17 +39,20 @@
     n_space, n_help,
     x_hbm, src_hbm, tgt_hbm, ang_hbm, env_hbm, live_ref, w0_hbm, w1_hbm, w2_hbm,
     out_ref,
-    src_ref, tgt_ref, ang_ref, env_ref, live_at, xv, rx_one, rx_two, rx_zero, edges,
-    tx_one, tx_two, tx_zero, in_one, in_two, in_zero,
+    src_ref, tgt_ref, ang_ref, env_ref, live_at, xv, rx_one, rx_rest, edges,
+    tx_one, tx_rest, in_one, in_rest,
     wv_one, wv_two, wv_zero, give_one, give_two, give_zero, take_one, take_two, take_zero,
     x_sem, in_sem, w_sem, halo_send, halo_recv, edge_send, edge_recv,
     sum_send, sum_recv, out_send, out_recv,
 ):
     s, h, c = lax.axis_index("space"), lax.axis_index("help"), lax.axis_index("chan")
     has = ((h > 0, h < n_help - 1), (s > 0, s < n_space - 1))
-    rx = (rx_one, rx_two, rx_zero)
-    tx = (tx_one, tx_two, tx_zero)
-    sums_in = (in_one, in_two, in_zero)
+    rx_groups, tx_groups, in_groups = (rx_one, rx_rest), (tx_one, tx_rest), (in_one, in_rest)
+
+    def planes(one, rest):
+        return one, rest.at[:, :, 0:WIDTH[1]], rest.at[:, :, WIDTH[1]:WIDTH[1] + WIDTH[2]]
+
+    rx, tx, sums_in = planes(*rx_groups), planes(*tx_groups), planes(*in_groups)
     give = (give_one, give_two, give_zero)
     take = (take_one, take_two, take_zero)
     partner = (s, h, 1 - c)
@@ -96,7 +99,7 @@
 
     def halo_copy(plane, side):
         return pltpu.make_async_remote_copy(
-            src_ref=rx[plane].at[1], dst_ref=rx[plane].at[2 - 2 * side],
+            src_ref=rx_groups[plane].at[1], dst_ref=rx_groups[plane].at[2 - 2 * side],
             send_sem=halo_send.at[plane, side], recv_sem=halo_recv.at[plane, 1 - side],
             device_id=neighbour(FIRST[plane], side), device_id_type=MESH,
         )
@@ -113,7 +116,7 @@
 
     def sum_copy(plane, side):
         return pltpu.make_async_remote_copy(
-            src_ref=tx[plane].at[side], dst_ref=sums_in[plane].at[1 - side],
+            src_ref=tx_groups[plane].at[side], dst_ref=in_groups[plane].at[1 - side],
             send_sem=sum_send.at[plane, side], recv_sem=sum_recv.at[plane, 1 - side],
             device_id=neighbour(1 - FIRST[plane], side), device_id_type=MESH,
         )
@@ -140,11 +143,11 @@
             ref[1, :, pl.ds(128 * pair, 128)] = jnp.concatenate(
                 [xv[order[2 * pair]], xv[order[2 * pair + 1]]], axis=1
             )
-        for side in range(2):
+        for side in range(2) if plane != 1 else ():
 
             @pl.when(has[FIRST[plane]][side])
             def _():
-                halo_copy(plane, side).start()
+                halo_copy(min(plane, 1), side).start()
 
     for load in weights:
         load.start()
@@ -230,7 +233,7 @@
 
     own = []
     for plane in range(3):
-        for side in range(2):
+        for side in range(2) if plane != 2 else ():
 
             @pl.when(has[FIRST[plane]][side])
             def _():
@@ -241,9 +244,11 @@
         for side in range(2):
             tx[plane][side] = turned(plane, part[2 * side * rows:(2 * side + 1) * rows]).astype(BF16)
 
-            @pl.when(has[1 - FIRST[plane]][side])
-            def _():
-                sum_copy(plane, side).start()
+            if plane != 1:
+
+                @pl.when(has[1 - FIRST[plane]][side])
+                def _():
+                    sum_copy(min(plane, 1), side).start()
 
         own.append(turned(plane, part[rows:2 * rows]))
 
@@ -255,7 +260,7 @@
                 if axis == 1:
                     for copy in edge_copies(side):
                         copy.wait_send()
-                for plane in range(3):
+                for plane in range(2):
                     if FIRST[plane] == axis:
                         halo_copy(plane, side).wait_send()
 
@@ -275,7 +280,7 @@
     first_core = c == 0
     kept = []
     for plane in range(3):
-        for side in range(2):
+        for side in range(2) if plane != 2 else ():
 
             @pl.when(has[1 - FIRST[plane]][side])
             def _():
@@ -310,7 +315,7 @@
         kept.append(keep)
         out_copy(plane).start()
 
-    for plane in range(3):
+    for plane in range(2):
         for side in range(2):
 
             @pl.when(has[1 - FIRST[plane]][side])
@@ -348,15 +353,15 @@
                 *[pltpu.VMEM((3, 4, 128), kind) for kind in (jnp.int32, jnp.int32, F32, F32)],
                 pltpu.VMEM((3, 8, 128), jnp.int32),
                 pltpu.VMEM(feats.shape, BF16),
-                *[pltpu.VMEM((3, ATOMS, width), BF16) for width in WIDTH],
+                *[pltpu.VMEM((3, ATOMS, width), BF16) for width in (WIDTH[0], WIDTH[1] + WIDTH[2])],
                 pltpu.VMEM((3, 24, 128), F32),
-                *[pltpu.VMEM((2, ATOMS, width), BF16) for width in WIDTH + WIDTH],
+                *[pltpu.VMEM((2, ATOMS, width), BF16) for width in 2 * (WIDTH[0], WIDTH[1] + WIDTH[2])],
                 pltpu.VMEM((2, 6, HALF, 768), BF16),
                 pltpu.VMEM((2, 5, HALF, 640), BF16),
                 pltpu.VMEM((7, HALF, 896), BF16),
                 *[pltpu.VMEM((ATOMS, width), BF16) for width in GIVEN + GIVEN],
-                dma((6,)), dma((4,)), dma((3,)), dma((3, 2)), dma((3, 2)), dma((2, 5)), dma((2, 5)),
-                dma((3, 2)), dma((3, 2)), dma((3,)), dma((3,)),
+                dma((6,)), dma((4,)), dma((3,)), dma((2, 2)), dma((2, 2)), dma((2, 5)), dma((2, 5)),
+                dma((2, 2)), dma((2, 2)), dma((3,)), dma((3,)),
             ],
             compiler_params=pltpu.CompilerParams(
                 collective_id=0, has_side_effects=True, vmem_limit_bytes=60 * 1024 * 1024

time: 22.1 us -> 22.4 us (1.014)
  Pallas kernels: 20.5 us -> 20.8 us
    pallas_call x1, Pallas kernels: 20.5 us -> 20.8 us  [shards(): pl.pallas_call(functools.partial(kernel, n_space, n_help), out_shape=pltp...]
where the time goes in v5:
time: 22.4 us; the launch traced here: 22.2 us
  Pallas kernels  20.8 us (93%)
  local copies, waits for them, and re-layouts  0.69 us (3%)
  between operations  0.66 us (3%)
    pallas_call x1, Pallas kernels, shards(): pl.pallas_call(functools.partial(kernel, n_space, n_help), out_shape=pltp...  20.8 us
    unnamed x1, local copies, waits for them, and re-layouts  0.69 us

profile of v5, /device:TPU:1, one launch (start us, length us, event | category | flops | bytes accessed | tf_op | source)
XLA Modules:
  0.0 22.2 jit_solution(964519406740723130)
XLA Ops:
  0.7 20.8 %edge_mix.1 = bf16[29,32,64]{2,1,0:T(8,128)(2,1)S(1)} custom-call(bf16[49,32,64]{2,1,0:T(8,128)(2,1)} %bitcast.3, s32[4,128]{1,0:T(4,128)} %src_hbm.1, s32[4,128]{1,0:T(4,128)} %tgt_hbm.1, f32[4,128]{1,0:T(4,128)} %ang_hbm.1, f32[4,128]{1,0:T(4,128)} %env_hbm.1, s32[1]{0:T(128)S(6)} %copy.12.live_ref, bf16[7,128,896]{2,1,0:T(8,128)(2,1)} %w0_hbm.1, ...), custom_call_target="tpu_custom_call" | custom-call | flops 402653184 | bytes 8388608 | tf_op jit(solution)/shard_map/edge_mix/pallas_call | solution.py:347
  21.5 0.7 %copy.11 = bf16[32,29,64]{2,0,1:T(8,128)(2,1)} copy(bf16[32,29,64]{2,0,1:T(8,128)(2,1)S(1)} %bitcast.2) | data formatting | bytes 237568

commit v6 on v4

--- a/solution.py
+++ b/solution.py
@@ -245,7 +245,8 @@
             def _():
                 sum_copy(plane, side).start()
 
-        own.append(turned(plane, part[rows:2 * rows]))
+        own.append(part[rows:2 * rows])
+    own = [turned(plane, part) for plane, part in enumerate(own)]
 
     for axis in range(2):
         for side in range(2):

time: 22.1 us -> 22.1 us (level)
  no operation moved by 1% of the time
where the time goes in v6:
time: 22.1 us; the launch traced here: 21.9 us
  Pallas kernels  20.5 us (93%)
  local copies, waits for them, and re-layouts  0.69 us (3%)
  between operations  0.66 us (3%)
    pallas_call x1, Pallas kernels, shards(): pl.pallas_call(functools.partial(kernel, n_space, n_help), out_shape=pltp...  20.5 us
    unnamed x1, local copies, waits for them, and re-layouts  0.69 us

profile of v6, /device:TPU:1, one launch (start us, length us, event | category | flops | bytes accessed | tf_op | source)
XLA Modules:
  0.0 21.9 jit_solution(4656420824942437974)
XLA Ops:
  0.7 20.5 %edge_mix.1 = bf16[29,32,64]{2,1,0:T(8,128)(2,1)S(1)} custom-call(bf16[49,32,64]{2,1,0:T(8,128)(2,1)} %bitcast.3, s32[4,128]{1,0:T(4,128)} %src_hbm.1, s32[4,128]{1,0:T(4,128)} %tgt_hbm.1, f32[4,128]{1,0:T(4,128)} %ang_hbm.1, f32[4,128]{1,0:T(4,128)} %env_hbm.1, s32[1]{0:T(128)S(6)} %copy.12.live_ref, bf16[7,128,896]{2,1,0:T(8,128)(2,1)} %w0_hbm.1, ...), custom_call_target="tpu_custom_call" | custom-call | flops 402653184 | bytes 8388608 | tf_op jit(solution)/shard_map/edge_mix/pallas_call | solution.py:343
  21.2 0.7 %copy.11 = bf16[32,29,64]{2,0,1:T(8,128)(2,1)} copy(bf16[32,29,64]{2,0,1:T(8,128)(2,1)S(1)} %bitcast.2) | data formatting | bytes 237568
